TPU v7x, 32 devices: a whole 2x2x4 slice. The times are simulated.
32 devices in a mesh: row: 4 (over y, core), col: 8 (over z, x).
Axes of the slice: x: 2, y: 2, z: 4, core: 2. Of those that a mesh axis runs over, the one named last changes fastest.
Arguments:
- particles: float32 [1024, 128], P('row'), may hold values from -4 to 4
- log_weights: float32 [1024], P('row'), may hold values from -8 to 8
- targets: float32 [3072, 128], P('col'), may hold values from -5 to 5
Outputs:
- new_particles: float32 [3072, 128], P(('col', 'row'))
All inputs are finite; a program needn't handle non-finite values.
Results may differ from a plain program's by a relative error of at most 0.005.
Values sent between devices are 32-bit elements; how exact they have to be, the bound alone decides.
A program may use at most 64 MiB of HBM per device.

v0:
```python
import functools
import math

import jax
import jax.numpy as jnp
from jax import lax
from jax.experimental import pallas as pl
from jax.experimental.pallas import tpu as pltpu
from jax.sharding import PartitionSpec as P

ITERS = 3


EPS = 0.01
MESH = pl.DeviceIdType.MESH
HIGHEST = lax.Precision.HIGHEST
LANES = 128
CHUNK = 64
GRANT = 55168 * 1024
PIECES = 2


def cost_tile(source, points):
    source_sq = jnp.sum(source * source, axis=1)
    points_sq = jnp.sum(points * points, axis=1)
    cross = jnp.dot(source, points.T, precision=HIGHEST, preferred_element_type=jnp.float32)
    return (source_sq[:, None] + points_sq[None, :] - 2.0 * cross) / source.shape[1]


def row_update(particles, log_weights, targets, col_pot, block_count, block_rows):
    maxima = []
    totals = []
    for index in range(block_count):
        source = particles[index * block_rows : (index + 1) * block_rows]
        scores = (col_pot[None, :] - cost_tile(source, targets)) / EPS
        top = jnp.max(scores, axis=1)
        maxima.append(top)
        totals.append(jnp.sum(jnp.exp(scores - top[:, None]), axis=1))
    local_top = jnp.concatenate(maxima)
    local_sum = jnp.concatenate(totals)
    top = lax.pmax(local_top, "col")
    summed = lax.psum(local_sum * jnp.exp(local_top - top), "col")
    return EPS * (log_weights - (top + jnp.log(summed)))


def col_update(particles, targets, row_pot, block_count, block_rows):
    width = targets.shape[0]
    top = jnp.full((width,), -1e30, jnp.float32)
    summed = jnp.zeros((width,), jnp.float32)
    for index in range(block_count):
        source = particles[index * block_rows : (index + 1) * block_rows]
        potential = row_pot[index * block_rows : (index + 1) * block_rows]
        scores = (potential[:, None] - cost_tile(source, targets)) / EPS
        fresh = jnp.maximum(top, jnp.max(scores, axis=0))
        summed = summed * jnp.exp(top - fresh) + jnp.sum(jnp.exp(scores - fresh[None, :]), axis=0)
        top = fresh
    global_top = lax.pmax(top, "row")
    summed = lax.psum(summed * jnp.exp(top - global_top), "row")
    return global_top + jnp.log(summed)


def per_device_large(particles, log_weights, targets):
    row_count = particles.shape[0]
    block_count = max(1, row_count // 512)
    block_rows = row_count // block_count
    log_count = math.log(targets.shape[0] * lax.axis_size("col"))
    col_pot = jnp.zeros((targets.shape[0],), jnp.float32)
    col_lse = col_pot
    row_pot = log_weights
    for iteration in range(ITERS):
        row_pot = row_update(particles, log_weights, targets, col_pot, block_count, block_rows)
        col_lse = col_update(particles, targets, row_pot, block_count, block_rows)
        col_pot = EPS * (-log_count - col_lse)
    particles_half = particles.astype(jnp.bfloat16)
    acc = jnp.zeros(
        (lax.axis_size("row") * (targets.shape[0] // lax.axis_size("row")), particles.shape[1]),
        jnp.float32,
    )
    for index in range(block_count):
        source = particles[index * block_rows : (index + 1) * block_rows]
        potential = row_pot[index * block_rows : (index + 1) * block_rows]
        plan = jnp.exp(
            (potential[:, None] - cost_tile(source, targets)) / EPS - col_lse[None, :]
        ).astype(jnp.bfloat16)
        source_half = particles_half[index * block_rows : (index + 1) * block_rows]
        acc = acc + lax.dot_general(
            plan, source_half, (((0,), (0,)), ((), ())), preferred_element_type=jnp.float32
        )
    return lax.psum_scatter(acc, "row", scatter_dimension=0, tiled=True)


def dot_minor(a, b, precision):
    return lax.dot_general(
        a, b, (((1,), (1,)), ((), ())), precision=precision, preferred_element_type=jnp.float32
    )


def split(values):
    high = values.astype(jnp.bfloat16)
    rest = values - high.astype(jnp.float32)
    middle = rest.astype(jnp.bfloat16)
    low = (rest - middle.astype(jnp.float32)).astype(jnp.bfloat16)
    return high, middle, low


def kernel(
    cols,
    x_hbm,
    w_hbm,
    y_hbm,
    out_ref,
    held,
    points,
    weights_ref,
    point_parts,
    source_half,
    tile,
    sums,
    tops,
    part1,
    part2,
    part3,
    pots,
    local_sem,
    pair_sem,
    far_sem,
    fwd_sem,
    pot_sem,
    part_sem,
):
    rows = 4
    row = lax.axis_index("row")
    col = lax.axis_index("col")
    side = lax.rem(row, 2)
    twin = row + 1 - 2 * side
    far = lax.rem(row + 2, rows)
    far_twin = lax.rem(twin + 2, rows)
    block, feature = x_hbm.shape
    width = y_hbm.shape[0]
    total = rows * block
    groups = block // LANES
    piece = block // PIECES

    load_x = pltpu.make_async_copy(x_hbm, held.at[0], local_sem.at[0])
    load_y = pltpu.make_async_copy(y_hbm, points, local_sem.at[1])
    load_w = pltpu.make_async_copy(w_hbm, weights_ref, local_sem.at[2])
    load_y.start()
    load_x.start()
    load_w.start()

    barrier = pltpu.get_barrier_semaphore()
    for peer in (twin, far, far_twin):
        pl.semaphore_signal(barrier, inc=1, device_id=(peer, col), device_id_type=MESH)
    for step in range(1, cols):
        pl.semaphore_signal(
            barrier, inc=1, device_id=(row, lax.rem(col + step, cols)), device_id_type=MESH
        )

    def send(src, dst, sems, index, device):
        copy = pltpu.make_async_remote_copy(
            src_ref=src,
            dst_ref=dst,
            send_sem=sems.at[0, index],
            recv_sem=sems.at[1, index],
            device_id=device,
            device_id_type=MESH,
        )
        copy.start()
        return copy

    pl.semaphore_wait(barrier, rows - 1 + cols - 1)
    far_copies = []
    for index in range(PIECES):
        span = pl.ds(index * piece, piece)
        far_copies.append(send(x_hbm.at[span], held.at[2, span], far_sem, index, (far, col)))
    pair_copy = send(x_hbm, held.at[1], pair_sem, 0, (twin, col))

    scale = 2.0 / (feature * EPS)
    half = 1.0 / (feature * EPS)
    load_y.wait()
    y = points[...]
    y_square = jnp.sum(y * y, axis=1, keepdims=True) * half
    high, middle, low = split(y * scale)
    for place, part in enumerate((high, middle, high, middle, high, low)):
        point_parts[:, place * feature : (place + 1) * feature] = part

    def score(slot, start=0, size=block):
        high, middle, low = split(held[slot, start : start + size])
        first_lane = slot * block + start
        source_half[first_lane : first_lane + size, :] = high
        source_parts = jnp.concatenate([high, high, middle, middle, low, high], axis=1)
        cross = dot_minor(point_parts[...], source_parts, None)
        tile[:, first_lane : first_lane + size] = cross - y_square

    def exchange(part, index):
        copies = []
        for step in range(1, cols):
            copies.append(
                send(
                    part.at[0],
                    part.at[step],
                    part_sem.at[index],
                    step,
                    (row, lax.rem(col + step, cols)),
                )
            )
        return copies

    load_x.wait()
    load_w.wait()
    score(0)
    source = held[0]
    square_parts = jnp.concatenate(split(source * source), axis=1)
    square = dot_minor(jnp.ones((16, 3 * feature), jnp.bfloat16), square_parts, None)[:1] * half
    own = tile[:, :block] - square
    top = jnp.max(own, axis=0, keepdims=True)
    lse = top + jnp.log(jnp.sum(jnp.exp(own - top), axis=0, keepdims=True))
    for group in range(groups):
        part1[0, group : group + 1, :] = lse[:, group * LANES : (group + 1) * LANES]

    first = exchange(part1, 0)

    pair_copy.wait_recv()
    score(1)
    forwards = []
    for index in range(PIECES):
        far_copies[index].wait_recv()
        span = pl.ds(index * piece, piece)
        forwards.append(send(held.at[2, span], held.at[3, span], fwd_sem, index, (twin, col)))
        if index == 0:
            for copy in first:
                copy.wait_recv()
            every = part1[:, :groups, :]
            top = jnp.max(every, axis=0)
            row_lse = top + jnp.log(jnp.sum(jnp.exp(every - top[None]), axis=0))
            weights = weights_ref[...]
            for group in range(groups):
                pots[0, group : group + 1, :] = (weights - row_lse)[group : group + 1] - square[
                    :, group * LANES : (group + 1) * LANES
                ]
            pots[0, groups : 2 * groups, :] = weights
            pot_copies = [
                send(pots.at[0], pots.at[slot], pot_sem, slot, (peer, col))
                for slot, peer in ((1, twin), (2, far), (3, far_twin))
            ]
        score(2, index * piece, piece)
    for index in range(PIECES):
        forwards[index].wait_recv()
        score(3, index * piece, piece)
    for copy in pot_copies:
        copy.wait_recv()

    def spread(compact):
        return jnp.concatenate(
            [jnp.broadcast_to(compact[g : g + 1, :], (8, LANES)) for g in range(rows * groups)],
            axis=1,
        )

    def gathered(first_row):
        return jnp.concatenate(
            [pots[slot, first_row : first_row + groups, :] for slot in range(rows)], axis=0
        )

    def chunk_at(index):
        return pl.ds(pl.multiple_of(index * CHUNK, CHUNK), CHUNK)

    def sweep(body):
        def step(index, carry):
            body(chunk_at(index))
            return carry

        lax.fori_loop(0, width // CHUNK, step, 0)

    def by_eight(values):
        return values.reshape(CHUNK // 8, 8, values.shape[-1])

    def across(chunk):
        return by_eight(jnp.concatenate([tops[chunk, :]] * (rows * groups), axis=1))

    def fold(values, combine):
        lanes = [values[..., g * LANES : (g + 1) * LANES] for g in range(rows * groups)]
        return functools.reduce(combine, lanes).reshape(CHUNK, LANES)

    row_pot = spread(gathered(0))[None]
    mass = jnp.exp(gathered(groups)) * float(width * cols)

    def largest(chunk):
        sums[chunk, :] = fold(by_eight(tile[chunk, :]) + row_pot, jnp.maximum)

    def entries(chunk):
        shifted = (by_eight(tile[chunk, :]) + row_pot) - across(chunk)
        values = jnp.exp(shifted)
        tile[chunk, :] = values.reshape(CHUNK, total)
        sums[chunk, :] = fold(values, jnp.add)

    def column_sums(factor):
        def body(chunk):
            sums[chunk, :] = fold(by_eight(tile[chunk, :]) * factor[None], jnp.add)

        sweep(body)

    def invert():
        inverse = 1.0 / jnp.sum(sums[...], axis=1, keepdims=True)
        tops[...] = jnp.broadcast_to(inverse, tops.shape)

    def row_sums(part):
        def step(index, acc):
            chunk = chunk_at(index)
            return acc + jnp.sum(by_eight(tile[chunk, :]) * across(chunk), axis=0)

        acc = lax.fori_loop(0, width // CHUNK, step, jnp.zeros((8, total), jnp.float32))
        summed = jnp.sum(acc, axis=0, keepdims=True)
        for g in range(rows * groups):
            part[0, g : g + 1, :] = summed[:, g * LANES : (g + 1) * LANES]

    def finish(copies, part):
        for copy in copies:
            copy.wait_recv()
        return spread(mass / jnp.sum(part[...], axis=0))

    sweep(largest)
    tops[...] = jnp.broadcast_to(jnp.max(sums[...], axis=1, keepdims=True), tops.shape)
    sweep(entries)
    invert()
    row_sums(part2)
    second = exchange(part2, 1)
    column_sums(finish(second, part2))
    invert()
    row_sums(part3)
    third = exchange(part3, 2)
    factor = finish(third, part3)

    share = width // rows
    mine = tile[pl.ds(pl.multiple_of(row * share, 8), share), :]
    mine = (mine.reshape(share // 8, 8, total) * factor[None]).reshape(share, total)
    plan = mine * (1.0 / jnp.sum(mine, axis=1, keepdims=True))
    out_ref[...] = jnp.dot(
        plan.astype(jnp.bfloat16), source_half[...], preferred_element_type=jnp.float32
    )

    for copy in far_copies + [pair_copy] + forwards + pot_copies + first + second + third:
        copy.wait_send()


def per_device_small(cols, particles, log_weights, targets):
    block, feature = particles.shape
    width = targets.shape[0]
    groups = block // LANES
    part = pltpu.VMEM((cols, 8, LANES), jnp.float32)
    hbm = pl.BlockSpec(memory_space=pltpu.HBM)
    vmem = pl.BlockSpec(memory_space=pltpu.VMEM)
    return pl.pallas_call(
        functools.partial(kernel, cols),
        out_shape=jax.ShapeDtypeStruct((width // 4, feature), jnp.float32),
        in_specs=[hbm, hbm, hbm],
        out_specs=vmem,
        scratch_shapes=[
            pltpu.VMEM((4, block, feature), jnp.float32),
            pltpu.VMEM((width, feature), jnp.float32),
            pltpu.VMEM((groups, LANES), jnp.float32),
            pltpu.VMEM((width, 6 * feature), jnp.bfloat16),
            pltpu.VMEM((4 * block, feature), jnp.bfloat16),
            pltpu.VMEM((width, 4 * block), jnp.float32),
            pltpu.VMEM((width, LANES), jnp.float32),
            pltpu.VMEM((width, LANES), jnp.float32),
            part,
            part,
            part,
            pltpu.VMEM((4, 8, LANES), jnp.float32),
            pltpu.SemaphoreType.DMA((3,)),
            pltpu.SemaphoreType.DMA((2, 1)),
            pltpu.SemaphoreType.DMA((2, PIECES)),
            pltpu.SemaphoreType.DMA((2, PIECES)),
            pltpu.SemaphoreType.DMA((2, 4)),
            pltpu.SemaphoreType.DMA((3, 2, cols)),
        ],
        compiler_params=pltpu.CompilerParams(
            collective_id=0, has_side_effects=True, vmem_limit_bytes=GRANT
        ),
    )(particles, log_weights.reshape(groups, LANES), targets)


def per_device(rows, cols, particles, log_weights, targets):
    block = particles.shape[0]
    width = targets.shape[0]
    if rows == 4 and block == 2 * LANES and width % CHUNK == 0 and width % 64 == 0 and width <= 1024:
        return per_device_small(cols, particles, log_weights, targets)
    return per_device_large(particles, log_weights, targets)


def solution(mesh):
    placed = (P("row", None), P("row"), P("col", None))
    return jax.shard_map(
        functools.partial(per_device, mesh.shape["row"], mesh.shape["col"]),
        mesh=mesh,
        in_specs=placed,
        out_specs=P(("col", "row"), None),
        check_vma=False,
    )
```

profile of v0, /device:TPU:0, one launch (start us, length us, event | category | flops | bytes accessed | tf_op | source)
XLA Modules:
  0.0 24.1 jit_solution(8836365490364515673)
XLA Ops:
  0.0 0.0 copy-start
  0.0 0.7 %copy-done = f32[256]{0:T(256)S(1)} copy-done((f32[256]{0:T(256)S(1)}, f32[256]{0:T(256)}, u32[]{:S(2)}) %copy-start) | copy-done | bytes 1048
  0.7 22.8 %shard_map.37 = f32[96,128]{1,0:T(8,128)S(1)} custom-call(f32[256,128]{1,0:T(8,128)} %x_hbm.1, f32[2,128]{1,0:T(2,128)S(1)} %bitcast.1, f32[384,128]{1,0:T(8,128)} %y_hbm.1), custom_call_target="tpu_custom_call" | custom-call | tf_op jit(solution)/shard_map/pallas_call | solution.py:352
  23.5 0.6 %copy.5 = f32[96,128]{1,0:T(8,128)} copy(f32[96,128]{1,0:T(8,128)S(1)} %shard_map.37) | data formatting | bytes 98304
Async XLA Ops:
  0.0 0.7 %copy-start = (f32[256]{0:T(256)S(1)}, f32[256]{0:T(256)}, u32[]{:S(2)}) copy-start(f32[256]{0:T(256)} %param.4) | copy-start | bytes 3076
where the time goes:
time: 24.2 us; the launch traced here: 24.1 us
  Pallas kernels  22.8 us (94%)
  local copies, waits for them, and re-layouts  1.3 us (5%)
    pallas_call x1, Pallas kernels, per_device_small(): pl.pallas_call(functools.partial(kernel, cols), out_shape=jax.ShapeDtypeS...  22.8 us
    unnamed x3, local copies, waits for them, and re-layouts  1.3 us

commit v1 on v0

--- a/solution.py
+++ b/solution.py
@@ -192,19 +192,38 @@
         cross = dot_minor(point_parts[...], source_parts, None)
         tile[:, first_lane : first_lane + size] = cross - y_square
 
-    def exchange(part, index):
+    upper = col // (cols // 2)
+    place = col + upper * (cols - 1 - 2 * col)
+    order = list(range(cols - 1, cols // 2 - 1, -1))
+    order += [lax.rem(place + step, cols // 2) for step in range(1, cols // 2)]
+    peers = [rank + upper * (cols - 1 - 2 * rank) for rank in order]
+
+    def exchange(part, index, size):
         copies = []
-        for step in range(1, cols):
+        for number, peer in enumerate(peers):
             copies.append(
-                send(
-                    part.at[0],
-                    part.at[step],
-                    part_sem.at[index],
-                    step,
-                    (row, lax.rem(col + step, cols)),
+                pltpu.make_async_remote_copy(
+                    src_ref=part.at[col, :size],
+                    dst_ref=part.at[col, :size],
+                    send_sem=part_sem.at[index, 0, number],
+                    recv_sem=part_sem.at[index, 1, col],
+                    device_id=(row, peer),
+                    device_id_type=MESH,
                 )
             )
+            copies[-1].start()
         return copies
+
+    def arrive(part, index, size):
+        for number, peer in enumerate(reversed(peers)):
+            pltpu.make_async_remote_copy(
+                src_ref=part.at[peer, :size],
+                dst_ref=part.at[peer, :size],
+                send_sem=part_sem.at[index, 0, number],
+                recv_sem=part_sem.at[index, 1, peer],
+                device_id=(row, peer),
+                device_id_type=MESH,
+            ).wait_recv()
 
     load_x.wait()
     load_w.wait()
@@ -216,9 +235,9 @@
     top = jnp.max(own, axis=0, keepdims=True)
     lse = top + jnp.log(jnp.sum(jnp.exp(own - top), axis=0, keepdims=True))
     for group in range(groups):
-        part1[0, group : group + 1, :] = lse[:, group * LANES : (group + 1) * LANES]
-
-    first = exchange(part1, 0)
+        part1[col, group : group + 1, :] = lse[:, group * LANES : (group + 1) * LANES]
+
+    first = exchange(part1, 0, groups)
 
     pair_copy.wait_recv()
     score(1)
@@ -228,8 +247,7 @@
         span = pl.ds(index * piece, piece)
         forwards.append(send(held.at[2, span], held.at[3, span], fwd_sem, index, (twin, col)))
         if index == 0:
-            for copy in first:
-                copy.wait_recv()
+            arrive(part1, 0, groups)
             every = part1[:, :groups, :]
             top = jnp.max(every, axis=0)
             row_lse = top + jnp.log(jnp.sum(jnp.exp(every - top[None]), axis=0))
@@ -240,13 +258,16 @@
                 ]
             pots[0, groups : 2 * groups, :] = weights
             pot_copies = [
-                send(pots.at[0], pots.at[slot], pot_sem, slot, (peer, col))
+                send(
+                    pots.at[0, : 2 * groups],
+                    pots.at[slot, : 2 * groups],
+                    pot_sem,
+                    slot,
+                    (peer, col),
+                )
                 for slot, peer in ((1, twin), (2, far), (3, far_twin))
             ]
         score(2, index * piece, piece)
-    for index in range(PIECES):
-        forwards[index].wait_recv()
-        score(3, index * piece, piece)
     for copy in pot_copies:
         copy.wait_recv()
 
@@ -278,14 +299,20 @@
         return by_eight(jnp.concatenate([tops[chunk, :]] * (rows * groups), axis=1))
 
     def fold(values, combine):
-        lanes = [values[..., g * LANES : (g + 1) * LANES] for g in range(rows * groups)]
+        lanes = [values[..., g * LANES : (g + 1) * LANES] for g in range(values.shape[-1] // LANES)]
         return functools.reduce(combine, lanes).reshape(CHUNK, LANES)
 
     row_pot = spread(gathered(0))[None]
     mass = jnp.exp(gathered(groups)) * float(width * cols)
 
+    known = (rows - 1) * block
+
     def largest(chunk):
-        sums[chunk, :] = fold(by_eight(tile[chunk, :]) + row_pot, jnp.maximum)
+        sums[chunk, :] = fold(by_eight(tile[chunk, :known]) + row_pot[..., :known], jnp.maximum)
+
+    def largest_rest(chunk):
+        rest = fold(by_eight(tile[chunk, known:]) + row_pot[..., known:], jnp.maximum)
+        sums[chunk, :] = jnp.maximum(sums[chunk, :], rest)
 
     def entries(chunk):
         shifted = (by_eight(tile[chunk, :]) + row_pot) - across(chunk)
@@ -311,24 +338,27 @@
         acc = lax.fori_loop(0, width // CHUNK, step, jnp.zeros((8, total), jnp.float32))
         summed = jnp.sum(acc, axis=0, keepdims=True)
         for g in range(rows * groups):
-            part[0, g : g + 1, :] = summed[:, g * LANES : (g + 1) * LANES]
-
-    def finish(copies, part):
-        for copy in copies:
-            copy.wait_recv()
+            part[col, g : g + 1, :] = summed[:, g * LANES : (g + 1) * LANES]
+
+    def finish(part, index):
+        arrive(part, index, rows * groups)
         return spread(mass / jnp.sum(part[...], axis=0))
 
     sweep(largest)
+    for index in range(PIECES):
+        forwards[index].wait_recv()
+        score(3, index * piece, piece)
+    sweep(largest_rest)
     tops[...] = jnp.broadcast_to(jnp.max(sums[...], axis=1, keepdims=True), tops.shape)
     sweep(entries)
     invert()
     row_sums(part2)
-    second = exchange(part2, 1)
-    column_sums(finish(second, part2))
+    second = exchange(part2, 1, rows * groups)
+    column_sums(finish(part2, 1))
     invert()
     row_sums(part3)
-    third = exchange(part3, 2)
-    factor = finish(third, part3)
+    third = exchange(part3, 2, rows * groups)
+    factor = finish(part3, 2)
 
     share = width // rows
     mine = tile[pl.ds(pl.multiple_of(row * share, 8), share), :]

time: 24.2 us -> 24.9 us (1.029)
  Pallas kernels: 22.8 us -> 23.4 us
    pallas_call x1, Pallas kernels: 22.8 us -> 23.4 us  [per_device_small(): pl.pallas_call(functools.partial(kernel, cols), out_shape=jax.ShapeDtypeS...]
where the time goes in v1:
time: 24.9 us; the launch traced here: 24.7 us
  Pallas kernels  23.4 us (94%)
  local copies, waits for them, and re-layouts  1.3 us (5%)
    pallas_call x1, Pallas kernels, per_device_small(): pl.pallas_call(functools.partial(kernel, cols), out_shape=jax.ShapeDtypeS...  23.4 us
    unnamed x3, local copies, waits for them, and re-layouts  1.3 us

profile of v1, /device:TPU:0, one launch (start us, length us, event | category | flops | bytes accessed | tf_op | source)
XLA Modules:
  0.0 24.7 jit_solution(10165837568509180623)
XLA Ops:
  0.0 0.0 copy-start
  0.0 0.7 %copy-done = f32[256]{0:T(256)S(1)} copy-done((f32[256]{0:T(256)S(1)}, f32[256]{0:T(256)}, u32[]{:S(2)}) %copy-start) | copy-done | bytes 1048
  0.7 23.4 %shard_map.37 = f32[96,128]{1,0:T(8,128)S(1)} custom-call(f32[256,128]{1,0:T(8,128)} %x_hbm.1, f32[2,128]{1,0:T(2,128)S(1)} %bitcast.1, f32[384,128]{1,0:T(8,128)} %y_hbm.1), custom_call_target="tpu_custom_call" | custom-call | tf_op jit(solution)/shard_map/pallas_call | solution.py:382
  24.1 0.6 %copy.5 = f32[96,128]{1,0:T(8,128)} copy(f32[96,128]{1,0:T(8,128)S(1)} %shard_map.37) | data formatting | bytes 98304
Async XLA Ops:
  0.0 0.7 %copy-start = (f32[256]{0:T(256)S(1)}, f32[256]{0:T(256)}, u32[]{:S(2)}) copy-start(f32[256]{0:T(256)} %param.4) | copy-start | bytes 3076

commit v2 on v0

--- a/solution.py
+++ b/solution.py
@@ -117,6 +117,7 @@
     tile,
     sums,
     tops,
+    squares,
     part1,
     part2,
     part3,
@@ -148,16 +149,26 @@
     load_x.start()
     load_w.start()
 
+    def each(count, body):
+        def step(index, carry):
+            body(index)
+            return carry
+
+        lax.fori_loop(0, count, step, 0)
+
     barrier = pltpu.get_barrier_semaphore()
+
+    def greet(peer_row, peer_col):
+        pl.semaphore_signal(
+            barrier, inc=1, device_id=(peer_row, peer_col), device_id_type=MESH
+        )
+
     for peer in (twin, far, far_twin):
-        pl.semaphore_signal(barrier, inc=1, device_id=(peer, col), device_id_type=MESH)
-    for step in range(1, cols):
-        pl.semaphore_signal(
-            barrier, inc=1, device_id=(row, lax.rem(col + step, cols)), device_id_type=MESH
-        )
-
-    def send(src, dst, sems, index, device):
-        copy = pltpu.make_async_remote_copy(
+        greet(peer, col)
+    each(cols - 1, lambda index: greet(row, lax.rem(col + index + 1, cols)))
+
+    def link(src, dst, sems, index, device):
+        return pltpu.make_async_remote_copy(
             src_ref=src,
             dst_ref=dst,
             send_sem=sems.at[0, index],
@@ -165,89 +176,115 @@
             device_id=device,
             device_id_type=MESH,
         )
-        copy.start()
-        return copy
+
+    def far_link(index):
+        span = pl.ds(index * piece, piece)
+        return link(x_hbm.at[span], held.at[2, span], far_sem, index, (far, col))
+
+    def forward_link(index):
+        span = pl.ds(index * piece, piece)
+        return link(held.at[2, span], held.at[3, span], fwd_sem, index, (twin, col))
+
+    pair_link = link(x_hbm, held.at[1], pair_sem, 0, (twin, col))
+    pot_links = [
+        link(pots.at[0], pots.at[slot], pot_sem, slot, (peer, col))
+        for slot, peer in ((1, twin), (2, far), (3, far_twin))
+    ]
+
+    def part_link(part, number, index):
+        return link(
+            part.at[0],
+            part.at[index + 1],
+            part_sem.at[number],
+            index + 1,
+            (row, lax.rem(col + index + 1, cols)),
+        )
+
+    def exchange(part, number):
+        each(cols - 1, lambda index: part_link(part, number, index).start())
+
+    def arrive(part, number):
+        each(cols - 1, lambda index: part_link(part, number, index).wait_recv())
 
     pl.semaphore_wait(barrier, rows - 1 + cols - 1)
-    far_copies = []
     for index in range(PIECES):
-        span = pl.ds(index * piece, piece)
-        far_copies.append(send(x_hbm.at[span], held.at[2, span], far_sem, index, (far, col)))
-    pair_copy = send(x_hbm, held.at[1], pair_sem, 0, (twin, col))
+        far_link(index).start()
+    pair_link.start()
 
     scale = 2.0 / (feature * EPS)
     half = 1.0 / (feature * EPS)
     load_y.wait()
-    y = points[...]
-    y_square = jnp.sum(y * y, axis=1, keepdims=True) * half
-    high, middle, low = split(y * scale)
-    for place, part in enumerate((high, middle, high, middle, high, low)):
-        point_parts[:, place * feature : (place + 1) * feature] = part
-
-    def score(slot, start=0, size=block):
-        high, middle, low = split(held[slot, start : start + size])
-        first_lane = slot * block + start
-        source_half[first_lane : first_lane + size, :] = high
+
+    def split_points(index):
+        chunk = pl.ds(pl.multiple_of(index * CHUNK, CHUNK), CHUNK)
+        y = points[chunk, :]
+        square = jnp.sum(y * y, axis=1, keepdims=True) * half
+        tops[chunk, :] = jnp.broadcast_to(square, (CHUNK, LANES))
+        high, middle, low = split(y * scale)
+        point_parts[chunk, :] = jnp.concatenate([high, middle, high, middle, high, low], axis=1)
+
+    each(width // CHUNK, split_points)
+    load_x.wait()
+    load_w.wait()
+
+    def score(slot):
+        high, middle, low = split(held[slot])
+        here = pl.ds(pl.multiple_of(slot * block, block), block)
+        source_half[here, :] = high
         source_parts = jnp.concatenate([high, high, middle, middle, low, high], axis=1)
         cross = dot_minor(point_parts[...], source_parts, None)
-        tile[:, first_lane : first_lane + size] = cross - y_square
-
-    def exchange(part, index):
-        copies = []
-        for step in range(1, cols):
-            copies.append(
-                send(
-                    part.at[0],
-                    part.at[step],
-                    part_sem.at[index],
-                    step,
-                    (row, lax.rem(col + step, cols)),
-                )
-            )
-        return copies
-
-    load_x.wait()
-    load_w.wait()
-    score(0)
-    source = held[0]
-    square_parts = jnp.concatenate(split(source * source), axis=1)
-    square = dot_minor(jnp.ones((16, 3 * feature), jnp.bfloat16), square_parts, None)[:1] * half
-    own = tile[:, :block] - square
-    top = jnp.max(own, axis=0, keepdims=True)
-    lse = top + jnp.log(jnp.sum(jnp.exp(own - top), axis=0, keepdims=True))
-    for group in range(groups):
-        part1[0, group : group + 1, :] = lse[:, group * LANES : (group + 1) * LANES]
-
-    first = exchange(part1, 0)
-
-    pair_copy.wait_recv()
-    score(1)
-    forwards = []
-    for index in range(PIECES):
-        far_copies[index].wait_recv()
-        span = pl.ds(index * piece, piece)
-        forwards.append(send(held.at[2, span], held.at[3, span], fwd_sem, index, (twin, col)))
-        if index == 0:
-            for copy in first:
-                copy.wait_recv()
-            every = part1[:, :groups, :]
-            top = jnp.max(every, axis=0)
-            row_lse = top + jnp.log(jnp.sum(jnp.exp(every - top[None]), axis=0))
-            weights = weights_ref[...]
-            for group in range(groups):
-                pots[0, group : group + 1, :] = (weights - row_lse)[group : group + 1] - square[
-                    :, group * LANES : (group + 1) * LANES
-                ]
-            pots[0, groups : 2 * groups, :] = weights
-            pot_copies = [
-                send(pots.at[0], pots.at[slot], pot_sem, slot, (peer, col))
-                for slot, peer in ((1, twin), (2, far), (3, far_twin))
-            ]
-        score(2, index * piece, piece)
-    for index in range(PIECES):
-        forwards[index].wait_recv()
-        score(3, index * piece, piece)
-    for copy in pot_copies:
+        tile[:, here] = cross - jnp.concatenate([tops[...]] * groups, axis=1)
+
+    def first_sums():
+        source = held[0]
+        square_parts = jnp.concatenate(split(source * source), axis=1)
+        square = dot_minor(jnp.ones((16, 3 * feature), jnp.bfloat16), square_parts, None)[:1] * half
+        own = tile[:, :block] - square
+        top = jnp.max(own, axis=0, keepdims=True)
+        lse = top + jnp.log(jnp.sum(jnp.exp(own - top), axis=0, keepdims=True))
+        for group in range(groups):
+            lanes = slice(group * LANES, (group + 1) * LANES)
+            part1[0, group : group + 1, :] = lse[:, lanes]
+            squares[group : group + 1, :] = square[:, lanes]
+        exchange(part1, 0)
+
+    def first_potential():
+        arrive(part1, 0)
+        every = part1[:, :groups, :]
+        top = jnp.max(every, axis=0)
+        row_lse = top + jnp.log(jnp.sum(jnp.exp(every - top[None]), axis=0))
+        weights = weights_ref[...]
+        pots[0, :groups, :] = weights - row_lse - squares[...]
+        pots[0, groups : 2 * groups, :] = weights
+        for copy in pot_links:
+            copy.start()
+
+    def take_block(slot):
+        @pl.when(slot == 1)
+        def _():
+            pair_link.wait_recv()
+
+        @pl.when(slot == 2)
+        def _():
+            for index in range(PIECES):
+                far_link(index).wait_recv()
+                forward_link(index).start()
+                if index == 0:
+                    first_potential()
+
+        @pl.when(slot == 3)
+        def _():
+            for index in range(PIECES):
+                forward_link(index).wait_recv()
+
+        score(slot)
+
+        @pl.when(slot == 0)
+        def _():
+            first_sums()
+
+    each(rows, take_block)
+    for copy in pot_links:
         copy.wait_recv()
 
     def spread(compact):
@@ -265,11 +302,7 @@
         return pl.ds(pl.multiple_of(index * CHUNK, CHUNK), CHUNK)
 
     def sweep(body):
-        def step(index, carry):
-            body(chunk_at(index))
-            return carry
-
-        lax.fori_loop(0, width // CHUNK, step, 0)
+        each(width // CHUNK, lambda index: body(chunk_at(index)))
 
     def by_eight(values):
         return values.reshape(CHUNK // 8, 8, values.shape[-1])
@@ -293,17 +326,11 @@
         tile[chunk, :] = values.reshape(CHUNK, total)
         sums[chunk, :] = fold(values, jnp.add)
 
-    def column_sums(factor):
-        def body(chunk):
-            sums[chunk, :] = fold(by_eight(tile[chunk, :]) * factor[None], jnp.add)
-
-        sweep(body)
-
     def invert():
         inverse = 1.0 / jnp.sum(sums[...], axis=1, keepdims=True)
         tops[...] = jnp.broadcast_to(inverse, tops.shape)
 
-    def row_sums(part):
+    def row_sums(part, number):
         def step(index, acc):
             chunk = chunk_at(index)
             return acc + jnp.sum(by_eight(tile[chunk, :]) * across(chunk), axis=0)
@@ -312,34 +339,43 @@
         summed = jnp.sum(acc, axis=0, keepdims=True)
         for g in range(rows * groups):
             part[0, g : g + 1, :] = summed[:, g * LANES : (g + 1) * LANES]
-
-    def finish(copies, part):
-        for copy in copies:
-            copy.wait_recv()
-        return spread(mass / jnp.sum(part[...], axis=0))
+        exchange(part, number)
+
+    def finish(part, number):
+        arrive(part, number)
+        return spread(mass / jnp.sum(part[...], axis=0))[None]
 
     sweep(largest)
     tops[...] = jnp.broadcast_to(jnp.max(sums[...], axis=1, keepdims=True), tops.shape)
     sweep(entries)
     invert()
-    row_sums(part2)
-    second = exchange(part2, 1)
-    column_sums(finish(second, part2))
+    row_sums(part2, 1)
+    factor = finish(part2, 1)
+
+    def column_sums(chunk):
+        sums[chunk, :] = fold(by_eight(tile[chunk, :]) * factor, jnp.add)
+
+    sweep(column_sums)
     invert()
-    row_sums(part3)
-    third = exchange(part3, 2)
-    factor = finish(third, part3)
+    row_sums(part3, 2)
+    last_factor = finish(part3, 2)
 
     share = width // rows
     mine = tile[pl.ds(pl.multiple_of(row * share, 8), share), :]
-    mine = (mine.reshape(share // 8, 8, total) * factor[None]).reshape(share, total)
+    mine = (mine.reshape(share // 8, 8, total) * last_factor).reshape(share, total)
     plan = mine * (1.0 / jnp.sum(mine, axis=1, keepdims=True))
     out_ref[...] = jnp.dot(
         plan.astype(jnp.bfloat16), source_half[...], preferred_element_type=jnp.float32
     )
 
-    for copy in far_copies + [pair_copy] + forwards + pot_copies + first + second + third:
+    for index in range(PIECES):
+        far_link(index).wait_send()
+        forward_link(index).wait_send()
+    pair_link.wait_send()
+    for copy in pot_links:
         copy.wait_send()
+    for number, part in enumerate((part1, part2, part3)):
+        each(cols - 1, lambda index: part_link(part, number, index).wait_send())
 
 
 def per_device_small(cols, particles, log_weights, targets):
@@ -363,6 +399,7 @@
             pltpu.VMEM((width, 4 * block), jnp.float32),
             pltpu.VMEM((width, LANES), jnp.float32),
             pltpu.VMEM((width, LANES), jnp.float32),
+            pltpu.VMEM((groups, LANES), jnp.float32),
             part,
             part,
             part,

time: 24.2 us -> 24.8 us (1.025)
  Pallas kernels: 22.8 us -> 23.4 us
    pallas_call x1, Pallas kernels: 22.8 us -> 23.4 us  [per_device_small(): pl.pallas_call(functools.partial(kernel, cols), out_shape=jax.ShapeDtypeS...]
where the time goes in v2:
time: 24.8 us; the launch traced here: 24.7 us
  Pallas kernels  23.4 us (94%)
  local copies, waits for them, and re-layouts  1.3 us (5%)
    pallas_call x1, Pallas kernels, per_device_small(): pl.pallas_call(functools.partial(kernel, cols), out_shape=jax.ShapeDtypeS...  23.4 us
    unnamed x3, local copies, waits for them, and re-layouts  1.3 us

profile of v2, /device:TPU:0, one launch (start us, length us, event | category | flops | bytes accessed | tf_op | source)
XLA Modules:
  0.0 24.7 jit_solution(3352103569660324271)
XLA Ops:
  0.0 0.0 copy-start
  0.0 0.7 %copy-done = f32[256]{0:T(256)S(1)} copy-done((f32[256]{0:T(256)S(1)}, f32[256]{0:T(256)}, u32[]{:S(2)}) %copy-start) | copy-done | bytes 1048
  0.7 23.4 %shard_map.37 = f32[96,128]{1,0:T(8,128)S(1)} custom-call(f32[256,128]{1,0:T(8,128)} %x_hbm.1, f32[2,128]{1,0:T(2,128)S(1)} %bitcast.1, f32[384,128]{1,0:T(8,128)} %y_hbm.1), custom_call_target="tpu_custom_call" | custom-call | tf_op jit(solution)/shard_map/pallas_call | solution.py:388
  24.0 0.6 %copy.5 = f32[96,128]{1,0:T(8,128)} copy(f32[96,128]{1,0:T(8,128)S(1)} %shard_map.37) | data formatting | bytes 98304
Async XLA Ops:
  0.0 0.7 %copy-start = (f32[256]{0:T(256)S(1)}, f32[256]{0:T(256)}, u32[]{:S(2)}) copy-start(f32[256]{0:T(256)} %param.4) | copy-start | bytes 3076

commit v3 on v0

--- a/solution.py
+++ b/solution.py
@@ -181,24 +181,24 @@
     y = points[...]
     y_square = jnp.sum(y * y, axis=1, keepdims=True) * half
     high, middle, low = split(y * scale)
-    for place, part in enumerate((high, middle, high, middle, high, low)):
+    for place, part in enumerate((high, middle, high, middle)):
         point_parts[:, place * feature : (place + 1) * feature] = part
 
     def score(slot, start=0, size=block):
         high, middle, low = split(held[slot, start : start + size])
         first_lane = slot * block + start
         source_half[first_lane : first_lane + size, :] = high
-        source_parts = jnp.concatenate([high, high, middle, middle, low, high], axis=1)
+        source_parts = jnp.concatenate([high, high, middle, middle], axis=1)
         cross = dot_minor(point_parts[...], source_parts, None)
         tile[:, first_lane : first_lane + size] = cross - y_square
 
-    def exchange(part, index):
+    def exchange(part, index, size):
         copies = []
         for step in range(1, cols):
             copies.append(
                 send(
-                    part.at[0],
-                    part.at[step],
+                    part.at[0, :size],
+                    part.at[step, :size],
                     part_sem.at[index],
                     step,
                     (row, lax.rem(col + step, cols)),
@@ -218,7 +218,7 @@
     for group in range(groups):
         part1[0, group : group + 1, :] = lse[:, group * LANES : (group + 1) * LANES]
 
-    first = exchange(part1, 0)
+    first = exchange(part1, 0, groups)
 
     pair_copy.wait_recv()
     score(1)
@@ -239,8 +239,9 @@
                     :, group * LANES : (group + 1) * LANES
                 ]
             pots[0, groups : 2 * groups, :] = weights
+            used = 2 * groups
             pot_copies = [
-                send(pots.at[0], pots.at[slot], pot_sem, slot, (peer, col))
+                send(pots.at[0, :used], pots.at[slot, :used], pot_sem, slot, (peer, col))
                 for slot, peer in ((1, twin), (2, far), (3, far_twin))
             ]
         score(2, index * piece, piece)
@@ -269,7 +270,7 @@
             body(chunk_at(index))
             return carry
 
-        lax.fori_loop(0, width // CHUNK, step, 0)
+        lax.fori_loop(0, width // CHUNK, step, 0, unroll=True)
 
     def by_eight(values):
         return values.reshape(CHUNK // 8, 8, values.shape[-1])
@@ -308,7 +309,9 @@
             chunk = chunk_at(index)
             return acc + jnp.sum(by_eight(tile[chunk, :]) * across(chunk), axis=0)
 
-        acc = lax.fori_loop(0, width // CHUNK, step, jnp.zeros((8, total), jnp.float32))
+        acc = lax.fori_loop(
+            0, width // CHUNK, step, jnp.zeros((8, total), jnp.float32), unroll=True
+        )
         summed = jnp.sum(acc, axis=0, keepdims=True)
         for g in range(rows * groups):
             part[0, g : g + 1, :] = summed[:, g * LANES : (g + 1) * LANES]
@@ -323,11 +326,11 @@
     sweep(entries)
     invert()
     row_sums(part2)
-    second = exchange(part2, 1)
+    second = exchange(part2, 1, rows * groups)
     column_sums(finish(second, part2))
     invert()
     row_sums(part3)
-    third = exchange(part3, 2)
+    third = exchange(part3, 2, rows * groups)
     factor = finish(third, part3)
 
     share = width // rows
@@ -358,7 +361,7 @@
             pltpu.VMEM((4, block, feature), jnp.float32),
             pltpu.VMEM((width, feature), jnp.float32),
             pltpu.VMEM((groups, LANES), jnp.float32),
-            pltpu.VMEM((width, 6 * feature), jnp.bfloat16),
+            pltpu.VMEM((width, 4 * feature), jnp.bfloat16),
             pltpu.VMEM((4 * block, feature), jnp.bfloat16),
             pltpu.VMEM((width, 4 * block), jnp.float32),
             pltpu.VMEM((width, LANES), jnp.float32),

time: 24.2 us -> 23.6 us (0.975)
  Pallas kernels: 22.8 us -> 22.1 us
    pallas_call x1, Pallas kernels: 22.8 us -> 22.1 us  [per_device_small(): pl.pallas_call(functools.partial(kernel, cols), out_shape=jax.ShapeDtypeS...]
where the time goes in v3:
time: 23.6 us; the launch traced here: 23.4 us
  Pallas kernels  22.1 us (94%)
  local copies, waits for them, and re-layouts  1.3 us (6%)
    pallas_call x1, Pallas kernels, per_device_small(): pl.pallas_call(functools.partial(kernel, cols), out_shape=jax.ShapeDtypeS...  22.1 us
    unnamed x3, local copies, waits for them, and re-layouts  1.3 us

profile of v3, /device:TPU:0, one launch (start us, length us, event | category | flops | bytes accessed | tf_op | source)
XLA Modules:
  0.0 23.4 jit_solution(2443898738343656408)
XLA Ops:
  0.0 0.0 copy-start
  0.0 0.7 %copy-done = f32[256]{0:T(256)S(1)} copy-done((f32[256]{0:T(256)S(1)}, f32[256]{0:T(256)}, u32[]{:S(2)}) %copy-start) | copy-done | bytes 1048
  0.7 22.1 %shard_map.37 = f32[96,128]{1,0:T(8,128)S(1)} custom-call(f32[256,128]{1,0:T(8,128)} %x_hbm.1, f32[2,128]{1,0:T(2,128)S(1)} %bitcast.1, f32[384,128]{1,0:T(8,128)} %y_hbm.1), custom_call_target="tpu_custom_call" | custom-call | tf_op jit(solution)/shard_map/pallas_call | solution.py:355
  22.8 0.6 %copy.5 = f32[96,128]{1,0:T(8,128)} copy(f32[96,128]{1,0:T(8,128)S(1)} %shard_map.37) | data formatting | bytes 98304
Async XLA Ops:
  0.0 0.7 %copy-start = (f32[256]{0:T(256)S(1)}, f32[256]{0:T(256)}, u32[]{:S(2)}) copy-start(f32[256]{0:T(256)} %param.4) | copy-start | bytes 3076

commit v4 on v3

--- a/solution.py
+++ b/solution.py
@@ -212,9 +212,9 @@
     source = held[0]
     square_parts = jnp.concatenate(split(source * source), axis=1)
     square = dot_minor(jnp.ones((16, 3 * feature), jnp.bfloat16), square_parts, None)[:1] * half
-    own = tile[:, :block] - square
+    own = tile[:, :block]
     top = jnp.max(own, axis=0, keepdims=True)
-    lse = top + jnp.log(jnp.sum(jnp.exp(own - top), axis=0, keepdims=True))
+    lse = top + jnp.log(jnp.sum(jnp.exp(own - top), axis=0, keepdims=True)) - square
     for group in range(groups):
         part1[0, group : group + 1, :] = lse[:, group * LANES : (group + 1) * LANES]
 
@@ -244,10 +244,10 @@
                 send(pots.at[0, :used], pots.at[slot, :used], pot_sem, slot, (peer, col))
                 for slot, peer in ((1, twin), (2, far), (3, far_twin))
             ]
-        score(2, index * piece, piece)
+    score(2)
     for index in range(PIECES):
         forwards[index].wait_recv()
-        score(3, index * piece, piece)
+    score(3)
     for copy in pot_copies:
         copy.wait_recv()
 

time: 23.6 us -> 23.6 us (level)
  no operation moved by 1% of the time
where the time goes in v4:
time: 23.6 us; the launch traced here: 23.4 us
  Pallas kernels  22.1 us (94%)
  local copies, waits for them, and re-layouts  1.3 us (6%)
    pallas_call x1, Pallas kernels, per_device_small(): pl.pallas_call(functools.partial(kernel, cols), out_shape=jax.ShapeDtypeS...  22.1 us
    unnamed x3, local copies, waits for them, and re-layouts  1.3 us

profile of v4, /device:TPU:0, one launch (start us, length us, event | category | flops | bytes accessed | tf_op | source)
XLA Modules:
  0.0 23.4 jit_solution(15136645883956983650)
XLA Ops:
  0.0 0.0 copy-start
  0.0 0.7 %copy-done = f32[256]{0:T(256)S(1)} copy-done((f32[256]{0:T(256)S(1)}, f32[256]{0:T(256)}, u32[]{:S(2)}) %copy-start) | copy-done | bytes 1048
  0.7 22.1 %shard_map.37 = f32[96,128]{1,0:T(8,128)S(1)} custom-call(f32[256,128]{1,0:T(8,128)} %x_hbm.1, f32[2,128]{1,0:T(2,128)S(1)} %bitcast.1, f32[384,128]{1,0:T(8,128)} %y_hbm.1), custom_call_target="tpu_custom_call" | custom-call | tf_op jit(solution)/shard_map/pallas_call | solution.py:355
  22.8 0.6 %copy.5 = f32[96,128]{1,0:T(8,128)} copy(f32[96,128]{1,0:T(8,128)S(1)} %shard_map.37) | data formatting | bytes 98304
Async XLA Ops:
  0.0 0.7 %copy-start = (f32[256]{0:T(256)S(1)}, f32[256]{0:T(256)}, u32[]{:S(2)}) copy-start(f32[256]{0:T(256)} %param.4) | copy-start | bytes 3076

commit v5 on v4

--- a/solution.py
+++ b/solution.py
@@ -116,7 +116,6 @@
     source_half,
     tile,
     sums,
-    tops,
     part1,
     part2,
     part3,
@@ -275,8 +274,8 @@
     def by_eight(values):
         return values.reshape(CHUNK // 8, 8, values.shape[-1])
 
-    def across(chunk):
-        return by_eight(jnp.concatenate([tops[chunk, :]] * (rows * groups), axis=1))
+    def across(column):
+        return by_eight(jnp.broadcast_to(column, (CHUNK, total)))
 
     def fold(values, combine):
         lanes = [values[..., g * LANES : (g + 1) * LANES] for g in range(rows * groups)]
@@ -289,7 +288,8 @@
         sums[chunk, :] = fold(by_eight(tile[chunk, :]) + row_pot, jnp.maximum)
 
     def entries(chunk):
-        shifted = (by_eight(tile[chunk, :]) + row_pot) - across(chunk)
+        top = jnp.max(sums[chunk, :], axis=1, keepdims=True)
+        shifted = (by_eight(tile[chunk, :]) + row_pot) - across(top)
         values = jnp.exp(shifted)
         tile[chunk, :] = values.reshape(CHUNK, total)
         sums[chunk, :] = fold(values, jnp.add)
@@ -300,14 +300,11 @@
 
         sweep(body)
 
-    def invert():
-        inverse = 1.0 / jnp.sum(sums[...], axis=1, keepdims=True)
-        tops[...] = jnp.broadcast_to(inverse, tops.shape)
-
     def row_sums(part):
         def step(index, acc):
             chunk = chunk_at(index)
-            return acc + jnp.sum(by_eight(tile[chunk, :]) * across(chunk), axis=0)
+            inverse = 1.0 / jnp.sum(sums[chunk, :], axis=1, keepdims=True)
+            return acc + jnp.sum(by_eight(tile[chunk, :]) * across(inverse), axis=0)
 
         acc = lax.fori_loop(
             0, width // CHUNK, step, jnp.zeros((8, total), jnp.float32), unroll=True
@@ -322,13 +319,10 @@
         return spread(mass / jnp.sum(part[...], axis=0))
 
     sweep(largest)
-    tops[...] = jnp.broadcast_to(jnp.max(sums[...], axis=1, keepdims=True), tops.shape)
     sweep(entries)
-    invert()
     row_sums(part2)
     second = exchange(part2, 1, rows * groups)
     column_sums(finish(second, part2))
-    invert()
     row_sums(part3)
     third = exchange(part3, 2, rows * groups)
     factor = finish(third, part3)
@@ -365,7 +359,6 @@
             pltpu.VMEM((4 * block, feature), jnp.bfloat16),
             pltpu.VMEM((width, 4 * block), jnp.float32),
             pltpu.VMEM((width, LANES), jnp.float32),
-            pltpu.VMEM((width, LANES), jnp.float32),
             part,
             part,
             part,

time: 23.6 us -> 23.6 us (level)
  no operation moved by 1% of the time
where the time goes in v5:
time: 23.6 us; the launch traced here: 23.4 us
  Pallas kernels  22.1 us (94%)
  local copies, waits for them, and re-layouts  1.3 us (6%)
    pallas_call x1, Pallas kernels, per_device_small(): pl.pallas_call(functools.partial(kernel, cols), out_shape=jax.ShapeDtypeS...  22.1 us
    unnamed x3, local copies, waits for them, and re-layouts  1.3 us

profile of v5, /device:TPU:0, one launch (start us, length us, event | category | flops | bytes accessed | tf_op | source)
XLA Modules:
  0.0 23.4 jit_solution(15136645883956983650)
XLA Ops:
  0.0 0.0 copy-start
  0.0 0.7 %copy-done = f32[256]{0:T(256)S(1)} copy-done((f32[256]{0:T(256)S(1)}, f32[256]{0:T(256)}, u32[]{:S(2)}) %copy-start) | copy-done | bytes 1048
  0.7 22.1 %shard_map.37 = f32[96,128]{1,0:T(8,128)S(1)} custom-call(f32[256,128]{1,0:T(8,128)} %x_hbm.1, f32[2,128]{1,0:T(2,128)S(1)} %bitcast.1, f32[384,128]{1,0:T(8,128)} %y_hbm.1), custom_call_target="tpu_custom_call" | custom-call | tf_op jit(solution)/shard_map/pallas_call | solution.py:349
  22.8 0.6 %copy.5 = f32[96,128]{1,0:T(8,128)} copy(f32[96,128]{1,0:T(8,128)S(1)} %shard_map.37) | data formatting | bytes 98304
Async XLA Ops:
  0.0 0.7 %copy-start = (f32[256]{0:T(256)S(1)}, f32[256]{0:T(256)}, u32[]{:S(2)}) copy-start(f32[256]{0:T(256)} %param.4) | copy-start | bytes 3076
